TPU v7x, 128 devices: a whole 4x4x4 slice. The times are simulated.
128 devices in a mesh: role: 2 (over z_hi), gx: 8 (over y, z_lo), gy: 8 (over x, core).
Axes of the slice: x: 4, y: 4, z: 4 (z_hi: 2, z_lo: 2; z = z_hi * 2 + z_lo), core: 2. Of those that a mesh axis runs over, the one named last changes fastest.
Arguments:
- design: float32 [256, 256, 256], P(('gx', 'gy'), None, 'role'), may hold values from 0 to 1
- force: float32 [3, 128, 128, 256], P(None, 'gx', 'gy', 'role'), may hold values from -6 to 6
- clamped_dof_mask: int32 [3, 128, 128, 256], P(None, 'gx', 'gy', 'role'), may hold values 0 or 1
- stiffness: float32 [81, 81], replicated, may hold values from -1 to 70, as said below
Outputs:
- sensitivity: float32 [256, 256, 256], P(('gx', 'gy'), None, 'role')
- displacement: float32 [3, 128, 128, 256], P(None, 'gx', 'gy', 'role')
Inputs may be any that keep to these rules, and one draw needn't show every extreme that they name: `stiffness`: symmetric, and each diagonal entry exceeds the sum of the magnitudes of the other entries of its row.
All inputs are finite; a program needn't handle non-finite values. No bound on the sum of `clamped_dof_mask` on one device may be relied on, other than what follows from the above.
Results may differ from a plain program's by a relative error of at most 0.00013.
Values sent between devices are 32-bit elements; how exact they have to be, the bound alone decides.
A program may use at most 64 MiB of HBM per device.

v0:
```python
import jax
import jax.numpy as jnp
from jax import lax
from jax.sharding import Mesh
from jax.sharding import PartitionSpec as P

ITERS = 3
RADIUS = 2
GX_GY = ("gx_0", "gx_1", "gy_0", "gy_1")
ROLE_GX_GY = ("role", "gx_0", "gx_1", "gy_0", "gy_1")
GX = ("gx_0", "gx_1")
GY = ("gy_0", "gy_1")
sharpness = 4.0
threshold = 0.5
floor_stiff = 0.001


def with_halo(block, sides, width):
    for axis, dim in sides:
        count = lax.axis_size(axis)
        forward = [(i, i + 1) for i in range(count - 1)]
        backward = [(target, source) for source, target in forward]
        low = lax.ppermute(
            lax.slice_in_dim(block, block.shape[dim] - width, None, axis=dim), axis, forward
        )
        high = lax.ppermute(lax.slice_in_dim(block, 0, width, axis=dim), axis, backward)
        block = jnp.concatenate([low, block, high], axis=dim)
    return block


def over_axes(shard, axes):
    for axis in axes:
        shard = lax.psum(shard, axis)
    return shard


def hat_list():
    return [float(RADIUS + 1 - abs(shift_idx - RADIUS)) for shift_idx in range(2 * RADIUS + 1)]


def smooth_axis(padded, axis_num, length):
    result = None
    for offset_idx, weight in enumerate(hat_list()):
        portion = weight * lax.slice_in_dim(padded, offset_idx, offset_idx + length, axis=axis_num)
        result = portion if result is None else result + portion
    return result


def axis_count(start, length, extent):
    places = start + jnp.arange(length, dtype=jnp.int32)
    counted = jnp.zeros((length,), jnp.float32)
    for offset_idx, weight in enumerate(hat_list()):
        target = places + (offset_idx - RADIUS)
        inside = jnp.logical_and(target >= 0, target < extent)
        counted = counted + weight * inside.astype(jnp.float32)
    return counted


def slab_weight(shape):
    extent_x, extent_y, extent_z = shape
    along_x = axis_count(
        lax.axis_index(GX_GY) * extent_x, extent_x, extent_x * lax.axis_size(GX_GY)
    )
    along_y = axis_count(0, extent_y, extent_y)
    along_z = axis_count(
        lax.axis_index("role") * extent_z, extent_z, extent_z * lax.axis_size("role")
    )
    return along_x[:, None, None] * along_y[None, :, None] * along_z[None, None, :]


def slab_smooth(field):
    extent_x, extent_y, extent_z = field.shape
    padded = with_halo(field, (("role", 2), (GX_GY, 0)), RADIUS)
    padded = jnp.pad(padded, ((0, 0), (RADIUS, RADIUS), (0, 0)))
    return smooth_axis(smooth_axis(smooth_axis(padded, 2, extent_z), 1, extent_y), 0, extent_x)


def heaviside_projection(values):
    scaled = jnp.tanh(sharpness * threshold) + jnp.tanh(sharpness * (1.0 - threshold))
    return (jnp.tanh(sharpness * threshold) + jnp.tanh(sharpness * (values - threshold))) / scaled


def slope(values):
    scaled = jnp.tanh(sharpness * threshold) + jnp.tanh(sharpness * (1.0 - threshold))
    bent = jnp.tanh(sharpness * (values - threshold))
    return sharpness * (1.0 - bent * bent) / scaled


def element_mean(fine):
    count_x = fine.shape[0] // 4
    count_y = fine.shape[1] // 4
    count_z = fine.shape[2] // 2
    return fine.reshape(count_x, 4, count_y, 4, count_z, 2).mean(axis=(1, 3, 5))


def spread(elements):
    count_x, count_y, count_z = elements.shape
    widened = jnp.broadcast_to(
        elements[:, None, :, None, :, None], (count_x, 4, count_y, 4, count_z, 2)
    )
    return widened.reshape(4 * count_x, 4 * count_y, 2 * count_z)


def corner_table(node_len):
    elem_len = (node_len - 1) // 2
    nodes = jnp.arange(node_len, dtype=jnp.int32)[None, :, None]
    elems = jnp.arange(elem_len, dtype=jnp.int32)[None, None, :]
    corners = jnp.arange(3, dtype=jnp.int32)[:, None, None]
    return (nodes == 2 * elems + corners).astype(jnp.float32)


def fold_table(node_len):
    rows = jnp.arange(node_len + 2, dtype=jnp.int32)[:, None]
    cols = jnp.arange(node_len, dtype=jnp.int32)[None, :]
    target = jnp.clip(rows - 1, 0, node_len - 1)
    return (target == cols).astype(jnp.float32)


def split_axis(values, axis_num):
    half_len = (values.shape[axis_num] - 1) // 2
    pieces = [
        lax.slice_in_dim(values, corner, corner + 2 * half_len - 1, stride=2, axis=axis_num)
        for corner in range(3)
    ]
    return jnp.stack(pieces, axis=0)


def split_nodes(values):
    stacked = split_axis(values, 1)
    stacked = split_axis(stacked, 3)
    table = corner_table(values.shape[3])
    stacked = jnp.einsum(
        "baqxyk,ckg->cbaqxyg",
        stacked,
        table,
        precision=lax.Precision.HIGHEST,
        preferred_element_type=jnp.float32,
    )
    return stacked.reshape(81, -1)


def merge_axis(parts, axis_num):
    opening = parts[0]
    middle = parts[1]
    closing = parts[2]
    length = opening.shape[axis_num]
    before = [(0, 0)] * opening.ndim
    before[axis_num] = (0, 1)
    behind = [(0, 0)] * opening.ndim
    behind[axis_num] = (1, 0)
    evens = jnp.pad(opening, before) + jnp.pad(closing, behind)
    leading = lax.slice_in_dim(evens, 0, length, axis=axis_num)
    ending = lax.slice_in_dim(evens, length, length + 1, axis=axis_num)
    braided = jnp.stack([leading, middle], axis=axis_num + 1)
    new_shape = list(leading.shape)
    new_shape[axis_num] = 2 * length
    return jnp.concatenate([braided.reshape(new_shape), ending], axis=axis_num)


def merge_nodes(stiffness_product, element_shape):
    reshaped = stiffness_product.reshape((3, 3, 3, 3) + tuple(element_shape))
    table = corner_table(2 * element_shape[2] + 1)
    merged = jnp.einsum(
        "cbaqxyg,ckg->baqxyk",
        reshaped,
        table,
        precision=lax.Precision.HIGHEST,
        preferred_element_type=jnp.float32,
    )
    merged = merge_axis(merged, 3)
    return merge_axis(merged, 1)


def fold_axis(padded, axis_num):
    inner_len = padded.shape[axis_num] - 2
    below = lax.slice_in_dim(padded, 0, 1, axis=axis_num)
    above = lax.slice_in_dim(padded, inner_len + 1, inner_len + 2, axis=axis_num)
    lowest = lax.slice_in_dim(padded, 1, 2, axis=axis_num) + below
    highest = lax.slice_in_dim(padded, inner_len, inner_len + 1, axis=axis_num) + above
    centre = lax.slice_in_dim(padded, 2, inner_len, axis=axis_num)
    return jnp.concatenate([lowest, centre, highest], axis=axis_num)


def shared_sum(values):
    padded = with_halo(values, (("role", 3), (GX, 1), (GY, 2)), 1)
    folded = fold_axis(fold_axis(padded, 1), 2)
    table = fold_table(values.shape[3])
    return jnp.einsum(
        "qxyk,kn->qxyn",
        folded,
        table,
        precision=lax.Precision.HIGHEST,
        preferred_element_type=jnp.float32,
    )


def inner_sum(left, right):
    local_part = jnp.sum((left * right)[:, :-1, :-1, :-1])
    return over_axes(local_part, ROLE_GX_GY)


def conjugate_gradient_solve(operate, rhs):
    solution = jnp.zeros_like(rhs)
    residual = rhs
    direction = rhs
    current = inner_sum(residual, residual)
    for sweep in range(ITERS):
        applied = operate(direction)
        step_len = current / inner_sum(direction, applied)
        solution = solution + step_len * direction
        residual = residual - step_len * applied
        updated = inner_sum(residual, residual)
        direction = residual + updated / current * direction
        current = updated
    return solution


def on_device(design, force, clamped_dof_mask, stiffness):
    filter_weight_grid = slab_weight(design.shape)
    filtered = slab_smooth(design) / filter_weight_grid
    density_slab = element_mean(heaviside_projection(filtered))
    density = lax.all_to_all(density_slab, GY, split_axis=1, concat_axis=0, tiled=True)
    factor = floor_stiff + (1.0 - floor_stiff) * density**3
    behind = ((0, 0), (0, 1), (0, 1), (0, 1))
    owned = jnp.concatenate([force, (1 - clamped_dof_mask).astype(jnp.float32)], axis=0)
    shared = shared_sum(jnp.pad(owned, behind))
    free = shared[3:]
    rhs = free * shared[:3]
    scales = factor.reshape(-1)

    def operate(values):
        columns = split_nodes(free * values)
        stiffness_product = (
            jnp.dot(
                stiffness,
                columns,
                precision=lax.Precision.HIGHEST,
                preferred_element_type=jnp.float32,
            )
            * scales[None, :]
        )
        return free * shared_sum(merge_nodes(stiffness_product, factor.shape))

    solution = conjugate_gradient_solve(operate, rhs)
    columns = split_nodes(solution)
    energy = jnp.sum(
        columns
        * jnp.dot(
            stiffness, columns, precision=lax.Precision.HIGHEST, preferred_element_type=jnp.float32
        ),
        axis=0,
    ).reshape(factor.shape)
    element_grad = -3.0 * density**2 * (1.0 - floor_stiff) * energy / 32.0
    slab_grad = lax.all_to_all(element_grad, GY, split_axis=0, concat_axis=1, tiled=True)
    voxel_grad = spread(slab_grad) * slope(filtered)
    sensitivity = slab_smooth(voxel_grad / filter_weight_grid)
    return (sensitivity, solution[:, :-1, :-1, :-1])


def solution(mesh):
    torus = Mesh(
        mesh.devices.reshape(mesh.shape["role"], 4, 2, 4, 2),
        ("role", "gx_0", "gx_1", "gy_0", "gy_1"),
    )
    return jax.shard_map(
        on_device,
        mesh=torus,
        in_specs=(P(GX_GY, None, "role"), P(None, GX, GY, "role"), P(None, GX, GY, "role"), P()),
        out_specs=(P(GX_GY, None, "role"), P(None, GX, GY, "role")),
        check_vma=False,
    )
```

profile of v0, /device:TPU:39, one launch (start us, length us, event | category | flops | bytes accessed | tf_op | source)
XLA Modules:
  0.0 574.3 jit_solution(5358044814999670989)
XLA Ops:
  0.7 4.7 collective-permute-start.4
  17.8 9.4 %collective-permute-done.5 = f32[6,17,17,1]{2,3,1,0:T(1,128)S(1)} collective-permute-done((f32[6,17,17,1]{2,3,1,0:T(1,128)S(1)}, f32[6,17,17,1]{2,3,1,0:T(1,128)S(1)}, u32[]{:S(2)}, u32[]{:S(2)}) %collective-permute-start.5) | collective-permute-done | bytes 6968 | tf_op jit(solution)/shard_map/ppermute | solution.py:26
  30.3 3.8 collective-permute-start.6
  42.9 5.7 collective-permute-start.9
  51.6 4.1 collective-permute-start.3
  62.8 5.8 %slice.538 = f32[3,3,8,8,129]{4,3,2,1,0:T(8,128)} slice(f32[3,3,8,17,129]{4,3,2,1,0:T(8,128)} %pad_maximum_fusion.2), slice={[0:3:1], [0:3:1], [0:8:1], [2:17:2], [0:129:1]} | slice | bytes 594432 | tf_op jit(solution)/shard_map/slice | solution.py:122
  68.6 5.7 slice.537
  74.3 5.7 slice.536
  84.9 5.7 reduce_sum.80
  95.6 6.4 %all-to-all-start = ((f32[8,1,512]{2,1,0:T(1,128)}), f32[8,1,512]{2,1,0:T(1,128)S(1)}, u32[]{:S(2)}, u32[]{:S(2)}) async-start(f32[8,1,512]{2,1,0:T(1,128)} %reshape.284), calls=%async_computation | async-start | bytes 32768 | tf_op jit(solution)/shard_map/all_to_all | solution.py:222
  102.0 4.4 fusion.40
  111.7 3.9 fusion.3
  115.6 3.3 reshape.253
  135.7 4.3 collective-permute-done.11
  147.8 3.4 collective-permute-done.13
  152.9 5.8 %collective-permute-start.15 = (f32[3,19,1,131]{3,2,1,0:T(1,128)S(1)}, f32[3,19,1,131]{3,2,1,0:T(1,128)S(1)}, u32[]{:S(2)}, u32[]{:S(2)}) collective-permute-start(f32[3,19,1,131]{3,2,1,0:T(1,128)S(1)} %get-tuple-element.31), channel_id=1, source_target_pairs={{1,0},{2,1},{3,2},{4,3},{5,4},{6,5},{7,6},{9,8},{10,9},{11,10},{12... | collective-permute-start | bytes 89612 | tf_op jit(solution)/shard_map/ppermute | solution.py:26
  164.5 5.9 %all-reduce.19 = (f32[]{:T(128)}, f32[]{:T(128)}) all-reduce(f32[]{:T(128)} %get-tuple-element.3, f32[]{:T(128)} %get-tuple-element.2), channel_id=1, replica_groups=mesh['role'=2,'gx_0'=4,'gx_1'=2,'gy_0'=4,'gy_1'=2] {'role'}, use_global_device_ids=true, to_apply=%region_3.4 | all-reduce | flops 2 | bytes 16 | tf_op jit(solution)/shard_map/psum | solution.py:33
  170.5 7.9 %all-reduce.16 = (f32[]{:T(128)}, f32[]{:T(128)}) all-reduce(f32[]{:T(128)} %get-tuple-element.12, f32[]{:T(128)} %get-tuple-element.13), channel_id=1, replica_groups=mesh['role'=2,'gx_0'=4,'gx_1'=2,'gy_0'=4,'gy_1'=2] {'gx_0'}, use_global_device_ids=true, to_apply=%region_4.5 | all-reduce | flops 2 | bytes 16 | tf_op jit(solution)/shard_map/psum | solution.py:33
  178.4 4.4 all-reduce.18
  182.8 9.5 %all-reduce.15 = (f32[]{:T(128)}, f32[]{:T(128)}) all-reduce(f32[]{:T(128)} %get-tuple-element.10, f32[]{:T(128)} %get-tuple-element.11), channel_id=1, replica_groups=mesh['role'=2,'gx_0'=4,'gx_1'=2,'gy_0'=4,'gy_1'=2] {'gy_0'}, use_global_device_ids=true, to_apply=%region_6.7 | all-reduce | flops 2 | bytes 16 | tf_op jit(solution)/shard_map/psum | solution.py:33
  192.3 8.4 %all-reduce.17 = (f32[]{:T(128)}, f32[]{:T(128)}) all-reduce(f32[]{:T(128)} %get-tuple-element.4, f32[]{:T(128)} %get-tuple-element.5), channel_id=1, replica_groups=mesh['role'=2,'gx_0'=4,'gx_1'=2,'gy_0'=4,'gy_1'=2] {'gy_1'}, use_global_device_ids=true, to_apply=%region_7.8 | all-reduce | flops 2 | bytes 16 | tf_op jit(solution)/shard_map/psum | solution.py:33
  205.6 5.9 %psum.220 = f32[]{:T(128)} all-reduce(f32[]{:T(128)} %fusion.97), channel_id=1, replica_groups=mesh['role'=2,'gx_0'=4,'gx_1'=2,'gy_0'=4,'gy_1'=2] {'role'}, use_global_device_ids=true, to_apply=%region_15.16 | all-reduce | flops 1 | bytes 8 | tf_op jit(solution)/shard_map/psum | solution.py:33
  211.5 7.0 %psum.221 = f32[]{:T(128)} all-reduce(f32[]{:T(128)} %psum.220), channel_id=1, replica_groups=mesh['role'=2,'gx_0'=4,'gx_1'=2,'gy_0'=4,'gy_1'=2] {'gx_0'}, use_global_device_ids=true, to_apply=%region_16.17 | all-reduce | flops 1 | bytes 8 | tf_op jit(solution)/shard_map/psum | solution.py:33
  218.5 4.4 psum.222
  222.9 8.6 %psum.223 = f32[]{:T(128)} all-reduce(f32[]{:T(128)} %psum.222), channel_id=1, replica_groups=mesh['role'=2,'gx_0'=4,'gx_1'=2,'gy_0'=4,'gy_1'=2] {'gy_0'}, use_global_device_ids=true, to_apply=%region_18.19 | all-reduce | flops 1 | bytes 8 | tf_op jit(solution)/shard_map/psum | solution.py:33
  231.5 9.8 %psum.224 = f32[]{:T(128)} all-reduce(f32[]{:T(128)} %psum.223), channel_id=1, replica_groups=mesh['role'=2,'gx_0'=4,'gx_1'=2,'gy_0'=4,'gy_1'=2] {'gy_1'}, use_global_device_ids=true, to_apply=%region_19.20 | all-reduce | flops 1 | bytes 8 | tf_op jit(solution)/shard_map/psum | solution.py:33
  242.6 3.5 slice_multiply_fusion.26
  247.7 4.9 slice.572
  252.6 5.7 slice.571
  258.3 5.7 slice.570
  263.9 4.4 fusion.39
  271.6 3.9 fusion.2
  275.5 3.3 reshape.257
  295.9 4.3 collective-permute-done.17
  308.0 3.7 collective-permute-done.19
  313.4 5.9 %collective-permute-start.21 = (f32[3,19,1,131]{3,2,1,0:T(1,128)S(1)}, f32[3,19,1,131]{3,2,1,0:T(1,128)S(1)}, u32[]{:S(2)}, u32[]{:S(2)}) collective-permute-start(f32[3,19,1,131]{3,2,1,0:T(1,128)S(1)} %get-tuple-element.29), channel_id=1, source_target_pairs={{1,0},{2,1},{3,2},{4,3},{5,4},{6,5},{7,6},{9,8},{10,9},{11,10},{12... | collective-permute-start | bytes 89612 | tf_op jit(solution)/shard_map/ppermute | solution.py:26
  325.0 6.0 %psum.225 = f32[]{:T(128)} all-reduce(f32[]{:T(128)} %fusion.96), channel_id=1, replica_groups=mesh['role'=2,'gx_0'=4,'gx_1'=2,'gy_0'=4,'gy_1'=2] {'role'}, use_global_device_ids=true, to_apply=%region_21.22 | all-reduce | flops 1 | bytes 8 | tf_op jit(solution)/shard_map/psum | solution.py:33
  331.0 6.7 %psum.226 = f32[]{:T(128)} all-reduce(f32[]{:T(128)} %psum.225), channel_id=1, replica_groups=mesh['role'=2,'gx_0'=4,'gx_1'=2,'gy_0'=4,'gy_1'=2] {'gx_0'}, use_global_device_ids=true, to_apply=%region_22.23 | all-reduce | flops 1 | bytes 8 | tf_op jit(solution)/shard_map/psum | solution.py:33
  337.7 4.8 psum.227
  342.4 10.6 %psum.228 = f32[]{:T(128)} all-reduce(f32[]{:T(128)} %psum.227), channel_id=1, replica_groups=mesh['role'=2,'gx_0'=4,'gx_1'=2,'gy_0'=4,'gy_1'=2] {'gy_0'}, use_global_device_ids=true, to_apply=%region_24.25 | all-reduce | flops 1 | bytes 8 | tf_op jit(solution)/shard_map/psum | solution.py:33
  353.0 6.8 %psum.229 = f32[]{:T(128)} all-reduce(f32[]{:T(128)} %psum.228), channel_id=1, replica_groups=mesh['role'=2,'gx_0'=4,'gx_1'=2,'gy_0'=4,'gy_1'=2] {'gy_1'}, use_global_device_ids=true, to_apply=%region_25.26 | all-reduce | flops 1 | bytes 8 | tf_op jit(solution)/shard_map/psum | solution.py:33
  364.8 6.0 %psum.230 = f32[]{:T(128)} all-reduce(f32[]{:T(128)} %fusion.95), channel_id=1, replica_groups=mesh['role'=2,'gx_0'=4,'gx_1'=2,'gy_0'=4,'gy_1'=2] {'role'}, use_global_device_ids=true, to_apply=%region_27.28 | all-reduce | flops 1 | bytes 8 | tf_op jit(solution)/shard_map/psum | solution.py:33
  370.7 8.4 %psum.231 = f32[]{:T(128)} all-reduce(f32[]{:T(128)} %psum.230), channel_id=1, replica_groups=mesh['role'=2,'gx_0'=4,'gx_1'=2,'gy_0'=4,'gy_1'=2] {'gx_0'}, use_global_device_ids=true, to_apply=%region_28.29 | all-reduce | flops 1 | bytes 8 | tf_op jit(solution)/shard_map/psum | solution.py:33
  379.1 4.5 psum.232
  383.6 8.6 %psum.233 = f32[]{:T(128)} all-reduce(f32[]{:T(128)} %psum.232), channel_id=1, replica_groups=mesh['role'=2,'gx_0'=4,'gx_1'=2,'gy_0'=4,'gy_1'=2] {'gy_0'}, use_global_device_ids=true, to_apply=%region_30.31 | all-reduce | flops 1 | bytes 8 | tf_op jit(solution)/shard_map/psum | solution.py:33
  392.2 9.5 %psum.234 = f32[]{:T(128)} all-reduce(f32[]{:T(128)} %psum.233), channel_id=1, replica_groups=mesh['role'=2,'gx_0'=4,'gx_1'=2,'gy_0'=4,'gy_1'=2] {'gy_1'}, use_global_device_ids=true, to_apply=%region_31.32 | all-reduce | flops 1 | bytes 8 | tf_op jit(solution)/shard_map/psum | solution.py:33
  407.0 3.3 slice.605
  410.2 3.3 slice.604
  418.4 3.9 fusion.1
  434.8 4.3 collective-permute-done.23
  450.0 5.9 %collective-permute-start.27 = (f32[3,19,1,131]{3,2,1,0:T(1,128)S(1)}, f32[3,19,1,131]{3,2,1,0:T(1,128)S(1)}, u32[]{:S(2)}, u32[]{:S(2)}) collective-permute-start(f32[3,19,1,131]{3,2,1,0:T(1,128)S(1)} %get-tuple-element.27), channel_id=1, source_target_pairs={{1,0},{2,1},{3,2},{4,3},{5,4},{6,5},{7,6},{9,8},{10,9},{11,10},{12... | collective-permute-start | bytes 89612 | tf_op jit(solution)/shard_map/ppermute | solution.py:26
  460.6 5.9 %psum.235 = f32[]{:T(128)} all-reduce(f32[]{:T(128)} %fusion.94), channel_id=1, replica_groups=mesh['role'=2,'gx_0'=4,'gx_1'=2,'gy_0'=4,'gy_1'=2] {'role'}, use_global_device_ids=true, to_apply=%region_33.34 | all-reduce | flops 1 | bytes 8 | tf_op jit(solution)/shard_map/psum | solution.py:33
  466.5 6.6 %psum.236 = f32[]{:T(128)} all-reduce(f32[]{:T(128)} %psum.235), channel_id=1, replica_groups=mesh['role'=2,'gx_0'=4,'gx_1'=2,'gy_0'=4,'gy_1'=2] {'gx_0'}, use_global_device_ids=true, to_apply=%region_34.35 | all-reduce | flops 1 | bytes 8 | tf_op jit(solution)/shard_map/psum | solution.py:33
  473.1 4.7 psum.237
  477.8 10.5 %psum.238 = f32[]{:T(128)} all-reduce(f32[]{:T(128)} %psum.237), channel_id=1, replica_groups=mesh['role'=2,'gx_0'=4,'gx_1'=2,'gy_0'=4,'gy_1'=2] {'gy_0'}, use_global_device_ids=true, to_apply=%region_36.37 | all-reduce | flops 1 | bytes 8 | tf_op jit(solution)/shard_map/psum | solution.py:33
  488.3 6.7 %psum.239 = f32[]{:T(128)} all-reduce(f32[]{:T(128)} %psum.238), channel_id=1, replica_groups=mesh['role'=2,'gx_0'=4,'gx_1'=2,'gy_0'=4,'gy_1'=2] {'gy_1'}, use_global_device_ids=true, to_apply=%region_37.38 | all-reduce | flops 1 | bytes 8 | tf_op jit(solution)/shard_map/psum | solution.py:33
  499.7 3.3 slice.638
  511.1 3.3 fusion.41
  514.6 8.8 %all_to_all.21 = f32[8,1,512]{2,1,0:T(1,128)S(1)} all-to-all(f32[8,1,512]{2,1,0:T(1,128)S(1)} %reshape.286), channel_id=1, replica_groups=mesh['role'=2,'gx_0'=4,'gx_1'=2,'gy_0'=4,'gy_1'=2] {'gy_0','gy_1'}, dimensions={0} | all-to-all | bytes 32768 | tf_op jit(solution)/shard_map/all_to_all | solution.py:254
  526.9 5.0 mul.384
  535.3 9.2 %collective-permute-done.28 = f32[4,256,2]{2,1,0:T(8,128)S(1)} collective-permute-done((f32[4,256,2]{2,1,0:T(8,128)S(1)}, f32[4,256,2]{2,1,0:T(8,128)S(1)}, u32[]{:S(2)}, u32[]{:S(2)}) %collective-permute-start.28) | collective-permute-done | bytes 8224 | tf_op jit(solution)/shard_map/ppermute | solution.py:23
  544.5 5.3 collective-permute-done.29
  550.4 7.0 %collective-permute-start.30 = (f32[2,256,132]{2,1,0:T(8,128)S(1)}, f32[2,256,132]{2,1,0:T(8,128)S(1)}, u32[]{:S(2)}, u32[]{:S(2)}) collective-permute-start(f32[2,256,132]{2,1,0:T(8,128)S(1)} %get-tuple-element.86), channel_id=1, source_target_pairs={{0,1},{1,2},{2,3},{3,4},{4,5},{5,6},{6,7},{7,8},{8,9},{9,10},{10,1... | collective-permute-start | bytes 811016 | tf_op jit(solution)/shard_map/ppermute | solution.py:23
  563.5 7.4 %collective-permute-done.31 = f32[2,256,132]{2,1,0:T(8,128)S(1)} collective-permute-done((f32[2,256,132]{2,1,0:T(8,128)S(1)}, f32[2,256,132]{2,1,0:T(8,128)S(1)}, u32[]{:S(2)}, u32[]{:S(2)}) %collective-permute-start.31) | collective-permute-done | bytes 270368 | tf_op jit(solution)/shard_map/ppermute | solution.py:26
  (275 shorter events, 190.1 us)
Async XLA Ops:
  0.6 111.1 %copy-start = (f32[81,81]{1,0:T(8,128)S(1)}, f32[81,81]{1,0:T(8,128)}, u32[]{:S(2)}) copy-start(f32[81,81]{1,0:T(8,128)} %param.7) | copy-start | bytes 78736
  0.6 10.6 %copy-start.20 = (s32[3,16,16,128]{3,2,1,0:T(8,128)S(1)}, s32[3,16,16,128]{3,2,1,0:T(8,128)}, u32[]{:S(2)}) copy-start(s32[3,16,16,128]{3,2,1,0:T(8,128)} %param.6) | copy-start | bytes 1179652
  0.7 10.6 %copy-start.19 = (f32[3,16,16,128]{3,2,1,0:T(8,128)S(1)}, f32[3,16,16,128]{3,2,1,0:T(8,128)}, u32[]{:S(2)}) copy-start(f32[3,16,16,128]{3,2,1,0:T(8,128)} %param.5) | copy-start | bytes 1179652
  0.7 15.4 %collective-permute-start.4 = (f32[6,17,17,1]{2,3,1,0:T(1,128)S(1)}, f32[6,17,17,1]{2,3,1,0:T(1,128)S(1)}, u32[]{:S(2)}, u32[]{:S(2)}) collective-permute-start(f32[6,17,17,1]{2,3,1,0:T(1,128)S(1)} %slice.514), channel_id=1, source_target_pairs={{0,64},{1,65},{2,66},{3,67},{4,68},{5,69},{6,70},{7,71},{8,72},{9,... | collective-permute-start | bytes 20816 | tf_op jit(solution)/shard_map/ppermute | solution.py:23
  7.9 28.1 %collective-permute-start = (f32[4,256,2]{2,1,0:T(8,128)}, f32[4,256,2]{2,1,0:T(8,128)}, u32[]{:S(2)}, u32[]{:S(2)}) collective-permute-start(f32[4,256,2]{2,1,0:T(8,128)} %get-tuple-element.92), channel_id=1, source_target_pairs={{0,64},{1,65},{2,66},{3,67},{4,68},{5,69},{6,70},{7,71},{8,72},{9,... | collective-permute-start | bytes 24584 | tf_op jit(solution)/shard_map/ppermute | solution.py:23
  10.0 26.1 %collective-permute-start.1 = (f32[4,256,2]{2,1,0:T(8,128)}, f32[4,256,2]{2,1,0:T(8,128)}, u32[]{:S(2)}, u32[]{:S(2)}) collective-permute-start(f32[4,256,2]{2,1,0:T(8,128)} %get-tuple-element.93), channel_id=1, source_target_pairs={{64,0},{65,1},{66,2},{67,3},{68,4},{69,5},{70,6},{71,7},{72,8},{73... | collective-permute-start | bytes 24584 | tf_op jit(solution)/shard_map/ppermute | solution.py:26
  14.6 12.7 %collective-permute-start.5 = (f32[6,17,17,1]{2,3,1,0:T(1,128)S(1)}, f32[6,17,17,1]{2,3,1,0:T(1,128)S(1)}, u32[]{:S(2)}, u32[]{:S(2)}) collective-permute-start(f32[6,17,17,1]{2,3,1,0:T(1,128)S(1)} %copy.52), channel_id=1, source_target_pairs={{64,0},{65,1},{66,2},{67,3},{68,4},{69,5},{70,6},{71,7},{72,8},{73... | collective-permute-start | bytes 20816 | tf_op jit(solution)/shard_map/ppermute | solution.py:26
  29.0 7.0 %copy-start.13 = (f32[4,256,128]{2,1,0:T(8,128)S(1)}, f32[4,256,128]{2,1,0:T(8,128)}, u32[]{:S(2)}) copy-start(f32[4,256,128]{2,1,0:T(8,128)} %param.4) | copy-start | bytes 1572868
  30.3 10.6 %copy-start.1 = (f32[6,17,17,1]{3,2,1,0:T(8,128)S(1)}, f32[6,17,17,1]{3,2,1,0:T(8,128)}, u32[]{:S(2)}) copy-start(f32[6,17,17,1]{3,2,1,0:T(8,128)} %copy.53) | copy-start | bytes 20812
  30.3 10.6 %copy-start.2 = (f32[6,17,17,1]{3,2,1,0:T(8,128)S(1)}, f32[6,17,17,1]{3,2,1,0:T(8,128)}, u32[]{:S(2)}) copy-start(f32[6,17,17,1]{3,2,1,0:T(8,128)} %copy.54) | copy-start | bytes 20812
  30.3 7.4 %collective-permute-start.6 = (f32[6,1,17,131]{3,2,1,0:T(8,128)S(1)}, f32[6,1,17,131]{3,2,1,0:T(8,128)S(1)}, u32[]{:S(2)}, u32[]{:S(2)}) collective-permute-start(f32[6,1,17,131]{3,2,1,0:T(8,128)S(1)} %get-tuple-element.24), channel_id=1, source_target_pairs={{0,8},{8,16},{16,24},{24,32},{32,40},{40,48},{48,56},{1,9},{9,17},... | collective-permute-start | bytes 160352 | tf_op jit(solution)/shard_map/ppermute | solution.py:23
  34.1 6.8 %collective-permute-start.7 = (f32[6,1,17,131]{3,2,1,0:T(8,128)S(1)}, f32[6,1,17,131]{3,2,1,0:T(8,128)S(1)}, u32[]{:S(2)}, u32[]{:S(2)}) collective-permute-start(f32[6,1,17,131]{3,2,1,0:T(8,128)S(1)} %get-tuple-element.25), channel_id=1, source_target_pairs={{8,0},{16,8},{24,16},{32,24},{40,32},{48,40},{56,48},{9,1},{17,9},... | collective-permute-start | bytes 160352 | tf_op jit(solution)/shard_map/ppermute | solution.py:26
  41.6 14.1 %collective-permute-start.8 = (f32[6,19,1,131]{3,2,1,0:T(1,128)S(1)}, f32[6,19,1,131]{3,2,1,0:T(1,128)S(1)}, u32[]{:S(2)}, u32[]{:S(2)}) collective-permute-start(f32[6,19,1,131]{3,2,1,0:T(1,128)S(1)} %get-tuple-element.22), channel_id=1, source_target_pairs={{0,1},{1,2},{2,3},{3,4},{4,5},{5,6},{6,7},{8,9},{9,10},{10,11},{11... | collective-permute-start | bytes 179216 | tf_op jit(solution)/shard_map/ppermute | solution.py:23
  42.9 12.8 %collective-permute-start.9 = (f32[6,19,1,131]{3,2,1,0:T(1,128)S(1)}, f32[6,19,1,131]{3,2,1,0:T(1,128)S(1)}, u32[]{:S(2)}, u32[]{:S(2)}) collective-permute-start(f32[6,19,1,131]{3,2,1,0:T(1,128)S(1)} %get-tuple-element.23), channel_id=1, source_target_pairs={{1,0},{2,1},{3,2},{4,3},{5,4},{6,5},{7,6},{9,8},{10,9},{11,10},{12... | collective-permute-start | bytes 179216 | tf_op jit(solution)/shard_map/ppermute | solution.py:26
  49.7 30.3 %collective-permute-start.2 = (f32[2,256,132]{2,1,0:T(8,128)}, f32[2,256,132]{2,1,0:T(8,128)}, u32[]{:S(2)}, u32[]{:S(2)}) collective-permute-start(f32[2,256,132]{2,1,0:T(8,128)} %get-tuple-element.88), channel_id=1, source_target_pairs={{0,1},{1,2},{2,3},{3,4},{4,5},{5,6},{6,7},{7,8},{8,9},{9,10},{10,1... | collective-permute-start | bytes 811016 | tf_op jit(solution)/shard_map/ppermute | solution.py:23
  51.6 28.4 %collective-permute-start.3 = (f32[2,256,132]{2,1,0:T(8,128)}, f32[2,256,132]{2,1,0:T(8,128)}, u32[]{:S(2)}, u32[]{:S(2)}) collective-permute-start(f32[2,256,132]{2,1,0:T(8,128)} %get-tuple-element.89), channel_id=1, source_target_pairs={{1,0},{2,1},{3,2},{4,3},{5,4},{6,5},{7,6},{8,7},{9,8},{10,9},{11,1... | collective-permute-start | bytes 811016 | tf_op jit(solution)/shard_map/ppermute | solution.py:26
  90.6 11.4 %copy-start.17 = (f32[3,3,8,8,129]{4,3,2,1,0:T(8,128)S(1)}, f32[3,3,8,8,129]{4,3,2,1,0:T(8,128)}, u32[]{:S(2)}) copy-start(f32[3,3,8,8,129]{4,3,2,1,0:T(8,128)} %slice.538) | copy-start | bytes 891652
  95.6 14.0 %all-to-all-start = ((f32[8,1,512]{2,1,0:T(1,128)}), f32[8,1,512]{2,1,0:T(1,128)S(1)}, u32[]{:S(2)}, u32[]{:S(2)}) async-start(f32[8,1,512]{2,1,0:T(1,128)} %reshape.284), calls=%async_computation | async-start | bytes 32768 | tf_op jit(solution)/shard_map/all_to_all | solution.py:222
  128.8 1.0 copy-start.3
  132.2 3.0 collective-permute-start.10
  133.9 6.1 %collective-permute-start.11 = (f32[3,17,17,1]{2,3,1,0:T(1,128)S(1)}, f32[3,17,17,1]{2,3,1,0:T(1,128)S(1)}, u32[]{:S(2)}, u32[]{:S(2)}) collective-permute-start(f32[3,17,17,1]{2,3,1,0:T(1,128)S(1)} %copy.64), channel_id=1, source_target_pairs={{64,0},{65,1},{66,2},{67,3},{68,4},{69,5},{70,6},{71,7},{72,8},{73... | collective-permute-start | bytes 10412 | tf_op jit(solution)/shard_map/ppermute | solution.py:26
  141.3 9.9 %copy-start.4 = (f32[3,8,2,17,129]{4,3,2,1,0:T(8,128)S(1)}, f32[3,8,2,17,129]{4,3,2,1,0:T(8,128)}, u32[]{:S(2)}) copy-start(f32[3,8,2,17,129]{4,3,2,1,0:T(8,128)} %copy-done.3) | copy-start | bytes 1263172
  141.3 9.9 %copy-start.10 = (f32[3,17,17,1]{3,2,1,0:T(8,128)S(1)}, f32[3,17,17,1]{3,2,1,0:T(8,128)}, u32[]{:S(2)}) copy-start(f32[3,17,17,1]{3,2,1,0:T(8,128)} %copy.66) | copy-start | bytes 10408
  142.4 5.3 collective-permute-start.12
  145.2 6.0 %collective-permute-start.13 = (f32[3,1,17,131]{3,2,1,0:T(8,128)S(1)}, f32[3,1,17,131]{3,2,1,0:T(8,128)S(1)}, u32[]{:S(2)}, u32[]{:S(2)}) collective-permute-start(f32[3,1,17,131]{3,2,1,0:T(8,128)S(1)} %get-tuple-element.38), channel_id=1, source_target_pairs={{8,0},{16,8},{24,16},{32,24},{40,32},{48,40},{56,48},{9,1},{17,9},... | collective-permute-start | bytes 80180 | tf_op jit(solution)/shard_map/ppermute | solution.py:26
  151.6 7.1 %collective-permute-start.14 = (f32[3,19,1,131]{3,2,1,0:T(1,128)S(1)}, f32[3,19,1,131]{3,2,1,0:T(1,128)S(1)}, u32[]{:S(2)}, u32[]{:S(2)}) collective-permute-start(f32[3,19,1,131]{3,2,1,0:T(1,128)S(1)} %get-tuple-element.30), channel_id=1, source_target_pairs={{0,1},{1,2},{2,3},{3,4},{4,5},{5,6},{6,7},{8,9},{9,10},{10,11},{11... | collective-permute-start | bytes 89612 | tf_op jit(solution)/shard_map/ppermute | solution.py:23
  152.9 6.6 %collective-permute-start.15 = (f32[3,19,1,131]{3,2,1,0:T(1,128)S(1)}, f32[3,19,1,131]{3,2,1,0:T(1,128)S(1)}, u32[]{:S(2)}, u32[]{:S(2)}) collective-permute-start(f32[3,19,1,131]{3,2,1,0:T(1,128)S(1)} %get-tuple-element.31), channel_id=1, source_target_pairs={{1,0},{2,1},{3,2},{4,3},{5,4},{6,5},{7,6},{9,8},{10,9},{11,10},{12... | collective-permute-start | bytes 89612 | tf_op jit(solution)/shard_map/ppermute | solution.py:26
  161.7 1.1 copy-start.15
  203.9 1.0 copy-start.9
  288.7 1.1 copy-start.5
  292.2 3.3 collective-permute-start.16
  294.2 6.1 %collective-permute-start.17 = (f32[3,17,17,1]{2,3,1,0:T(1,128)S(1)}, f32[3,17,17,1]{2,3,1,0:T(1,128)S(1)}, u32[]{:S(2)}, u32[]{:S(2)}) collective-permute-start(f32[3,17,17,1]{2,3,1,0:T(1,128)S(1)} %copy.76), channel_id=1, source_target_pairs={{64,0},{65,1},{66,2},{67,3},{68,4},{69,5},{70,6},{71,7},{72,8},{73... | collective-permute-start | bytes 10412 | tf_op jit(solution)/shard_map/ppermute | solution.py:26
  301.5 10.2 %copy-start.6 = (f32[3,8,2,17,129]{4,3,2,1,0:T(8,128)S(1)}, f32[3,8,2,17,129]{4,3,2,1,0:T(8,128)}, u32[]{:S(2)}) copy-start(f32[3,8,2,17,129]{4,3,2,1,0:T(8,128)} %copy-done.5) | copy-start | bytes 1263172
  301.5 10.2 %copy-start.11 = (f32[3,17,17,1]{3,2,1,0:T(8,128)S(1)}, f32[3,17,17,1]{3,2,1,0:T(8,128)}, u32[]{:S(2)}) copy-start(f32[3,17,17,1]{3,2,1,0:T(8,128)} %copy.78) | copy-start | bytes 10408
  302.7 5.3 collective-permute-start.18
  305.7 6.0 %collective-permute-start.19 = (f32[3,1,17,131]{3,2,1,0:T(8,128)S(1)}, f32[3,1,17,131]{3,2,1,0:T(8,128)S(1)}, u32[]{:S(2)}, u32[]{:S(2)}) collective-permute-start(f32[3,1,17,131]{3,2,1,0:T(8,128)S(1)} %get-tuple-element.36), channel_id=1, source_target_pairs={{8,0},{16,8},{24,16},{32,24},{40,32},{48,40},{56,48},{9,1},{17,9},... | collective-permute-start | bytes 80180 | tf_op jit(solution)/shard_map/ppermute | solution.py:26
  312.1 7.2 %collective-permute-start.20 = (f32[3,19,1,131]{3,2,1,0:T(1,128)S(1)}, f32[3,19,1,131]{3,2,1,0:T(1,128)S(1)}, u32[]{:S(2)}, u32[]{:S(2)}) collective-permute-start(f32[3,19,1,131]{3,2,1,0:T(1,128)S(1)} %get-tuple-element.28), channel_id=1, source_target_pairs={{0,1},{1,2},{2,3},{3,4},{4,5},{5,6},{6,7},{8,9},{9,10},{10,11},{11... | collective-permute-start | bytes 89612 | tf_op jit(solution)/shard_map/ppermute | solution.py:23
  313.4 6.6 %collective-permute-start.21 = (f32[3,19,1,131]{3,2,1,0:T(1,128)S(1)}, f32[3,19,1,131]{3,2,1,0:T(1,128)S(1)}, u32[]{:S(2)}, u32[]{:S(2)}) collective-permute-start(f32[3,19,1,131]{3,2,1,0:T(1,128)S(1)} %get-tuple-element.29), channel_id=1, source_target_pairs={{1,0},{2,1},{3,2},{4,3},{5,4},{6,5},{7,6},{9,8},{10,9},{11,10},{12... | collective-permute-start | bytes 89612 | tf_op jit(solution)/shard_map/ppermute | solution.py:26
  322.2 1.1 copy-start.16
  363.0 1.1 copy-start.14
  431.1 3.3 collective-permute-start.22
  433.1 6.1 %collective-permute-start.23 = (f32[3,17,17,1]{2,3,1,0:T(1,128)S(1)}, f32[3,17,17,1]{2,3,1,0:T(1,128)S(1)}, u32[]{:S(2)}, u32[]{:S(2)}) collective-permute-start(f32[3,17,17,1]{2,3,1,0:T(1,128)S(1)} %copy.88), channel_id=1, source_target_pairs={{64,0},{65,1},{66,2},{67,3},{68,4},{69,5},{70,6},{71,7},{72,8},{73... | collective-permute-start | bytes 10412 | tf_op jit(solution)/shard_map/ppermute | solution.py:26
  439.7 5.3 collective-permute-start.24
  442.2 6.0 %collective-permute-start.25 = (f32[3,1,17,131]{3,2,1,0:T(8,128)S(1)}, f32[3,1,17,131]{3,2,1,0:T(8,128)S(1)}, u32[]{:S(2)}, u32[]{:S(2)}) collective-permute-start(f32[3,1,17,131]{3,2,1,0:T(8,128)S(1)} %get-tuple-element.34), channel_id=1, source_target_pairs={{8,0},{16,8},{24,16},{32,24},{40,32},{48,40},{56,48},{9,1},{17,9},... | collective-permute-start | bytes 80180 | tf_op jit(solution)/shard_map/ppermute | solution.py:26
  448.7 7.3 %collective-permute-start.26 = (f32[3,19,1,131]{3,2,1,0:T(1,128)S(1)}, f32[3,19,1,131]{3,2,1,0:T(1,128)S(1)}, u32[]{:S(2)}, u32[]{:S(2)}) collective-permute-start(f32[3,19,1,131]{3,2,1,0:T(1,128)S(1)} %get-tuple-element.26), channel_id=1, source_target_pairs={{0,1},{1,2},{2,3},{3,4},{4,5},{5,6},{6,7},{8,9},{9,10},{10,11},{11... | collective-permute-start | bytes 89612 | tf_op jit(solution)/shard_map/ppermute | solution.py:23
  450.0 6.6 %collective-permute-start.27 = (f32[3,19,1,131]{3,2,1,0:T(1,128)S(1)}, f32[3,19,1,131]{3,2,1,0:T(1,128)S(1)}, u32[]{:S(2)}, u32[]{:S(2)}) collective-permute-start(f32[3,19,1,131]{3,2,1,0:T(1,128)S(1)} %get-tuple-element.27), channel_id=1, source_target_pairs={{1,0},{2,1},{3,2},{4,3},{5,4},{6,5},{7,6},{9,8},{10,9},{11,10},{12... | collective-permute-start | bytes 89612 | tf_op jit(solution)/shard_map/ppermute | solution.py:26
  457.8 38.6 %copy-start.7 = (f32[3,17,17,129]{3,2,1,0:T(8,128)S(1)}, f32[3,17,17,129]{3,2,1,0:T(8,128)}, u32[]{:S(2)}) copy-start(f32[3,17,17,129]{3,2,1,0:T(8,128)} %get-tuple-element.21) | copy-start | bytes 1342120
  457.8 38.6 %copy-start.8 = (f32[3,17,17,129]{3,2,1,0:T(8,128)S(1)}, f32[3,17,17,129]{3,2,1,0:T(8,128)}, u32[]{:S(2)}) copy-start(f32[3,17,17,129]{3,2,1,0:T(8,128)} %get-tuple-element.17) | copy-start | bytes 1342120
  498.0 1.0 copy-start.12
  526.9 5.1 copy-start.18
  532.4 12.1 %collective-permute-start.28 = (f32[4,256,2]{2,1,0:T(8,128)S(1)}, f32[4,256,2]{2,1,0:T(8,128)S(1)}, u32[]{:S(2)}, u32[]{:S(2)}) collective-permute-start(f32[4,256,2]{2,1,0:T(8,128)S(1)} %get-tuple-element.90), channel_id=1, source_target_pairs={{0,64},{1,65},{2,66},{3,67},{4,68},{5,69},{6,70},{7,71},{8,72},{9,... | collective-permute-start | bytes 24584 | tf_op jit(solution)/shard_map/ppermute | solution.py:23
  534.0 15.8 %collective-permute-start.29 = (f32[4,256,2]{2,1,0:T(8,128)S(1)}, f32[4,256,2]{2,1,0:T(8,128)S(1)}, u32[]{:S(2)}, u32[]{:S(2)}) collective-permute-start(f32[4,256,2]{2,1,0:T(8,128)S(1)} %get-tuple-element.91), channel_id=1, source_target_pairs={{64,0},{65,1},{66,2},{67,3},{68,4},{69,5},{70,6},{71,7},{72,8},{73... | collective-permute-start | bytes 24584 | tf_op jit(solution)/shard_map/ppermute | solution.py:26
  550.4 13.1 %collective-permute-start.30 = (f32[2,256,132]{2,1,0:T(8,128)S(1)}, f32[2,256,132]{2,1,0:T(8,128)S(1)}, u32[]{:S(2)}, u32[]{:S(2)}) collective-permute-start(f32[2,256,132]{2,1,0:T(8,128)S(1)} %get-tuple-element.86), channel_id=1, source_target_pairs={{0,1},{1,2},{2,3},{3,4},{4,5},{5,6},{6,7},{7,8},{8,9},{9,10},{10,1... | collective-permute-start | bytes 811016 | tf_op jit(solution)/shard_map/ppermute | solution.py:23
  557.4 13.5 %collective-permute-start.31 = (f32[2,256,132]{2,1,0:T(8,128)S(1)}, f32[2,256,132]{2,1,0:T(8,128)S(1)}, u32[]{:S(2)}, u32[]{:S(2)}) collective-permute-start(f32[2,256,132]{2,1,0:T(8,128)S(1)} %get-tuple-element.87), channel_id=1, source_target_pairs={{1,0},{2,1},{3,2},{4,3},{5,4},{6,5},{7,6},{8,7},{9,8},{10,9},{11,1... | collective-permute-start | bytes 811016 | tf_op jit(solution)/shard_map/ppermute | solution.py:26
where the time goes:
time: 581 us; the launch traced here: 574 us
  blocking collectives  187 us (32%)
  local copies, waits for them, and re-layouts  131 us (23%)
  starting transfers between devices  92 us (16%)
  waiting for transfers between devices  62.5 us (11%)
  other arithmetic  52.8 us (9%)
  matrix products  40.7 us (7%)
  between operations  9 us (2%)
    psum x25, blocking collectives, over_axes(): shard = lax.psum(shard, axis)  178 us
    ppermute x16, waiting for transfers between devices, with_halo(): lax.ppermute(lax.slice_in_dim(block, 0, width, axis=dim), axis, backward)  50.9 us
    slice x12, local copies, waits for them, and re-layouts, split_axis(): lax.slice_in_dim(values, corner, corner + 2 * half_len - 1, stride=2, axi...  47.5 us
    ppermute x16, starting transfers between devices, with_halo(): lax.ppermute(lax.slice_in_dim(block, 0, width, axis=dim), axis, backward)  46.6 us
    ppermute x16, starting transfers between devices, with_halo(): lax.ppermute(lax.slice_in_dim(block, block.shape[dim] - width, None, axis...  39 us
    dot_general x4, matrix products, split_nodes(): jnp.einsum('baqxyk,ckg->cbaqxyg', stacked, table, precision=lax.Precision...  14.6 us
    unnamed x54, local copies, waits for them, and re-layouts  12.2 us
    ppermute x16, waiting for transfers between devices, with_halo(): lax.ppermute(lax.slice_in_dim(block, block.shape[dim] - width, None, axis...  11.6 us
  transfers between devices with their start and end apart: 33, of which 15 were waited for; matrix products, arithmetic and copies ran while one was open for 9% of the time, Pallas kernels for 0%

commit v1 on v0

--- a/solution.py
+++ b/solution.py
@@ -30,7 +30,7 @@
 
 def over_axes(shard, axes):
     for axis in axes:
-        shard = lax.psum(shard, axis)
+        shard = jnp.sum(lax.all_gather(shard, axis), axis=0)
     return shard
 
 

time: 581 us -> 625 us (1.076)
  local copies, waits for them, and re-layouts: 131 us -> 173 us
  waiting for transfers between devices: 62.5 us -> 29.7 us
  starting transfers between devices: 92 us -> 114 us
  other arithmetic: 52.8 us -> 73.1 us
  blocking collectives: 187 us -> 173 us
    psum x25 -> x0, blocking collectives: 178 us -> none  [over_axes(): shard = lax.psum(shard, axis)]
    unnamed x0 -> x25, blocking collectives: none -> 164 us
    unnamed x54 -> x117, local copies, waits for them, and re-layouts: 12.2 us -> 57.6 us
    ppermute x16, waiting for transfers between devices: 50.9 us -> 12.5 us  [with_halo(): lax.ppermute(lax.slice_in_dim(block, 0, width, axis=dim), axis, backward)]
    ppermute x16, starting transfers between devices: 39 us -> 66.2 us  [with_halo(): lax.ppermute(lax.slice_in_dim(block, block.shape[dim] - width, None, axis...]
    reduce_sum x0 -> x30, other arithmetic: none -> 18.2 us  [over_axes(): shard = jnp.sum(lax.all_gather(shard, axis), axis=0)]
  transfers between devices with their start and end apart: 33 -> 33, of which waited for: 15 -> 14; matrix products, arithmetic and copies ran while one was open for 9% -> 8% of each run, Pallas kernels for 0% -> 0%
where the time goes in v1:
time: 625 us; the launch traced here: 614 us
  local copies, waits for them, and re-layouts  173 us (28%)
  blocking collectives  173 us (28%)
  starting transfers between devices  114 us (18%)
  other arithmetic  73.1 us (12%)
  matrix products  41.9 us (7%)
  waiting for transfers between devices  29.7 us (5%)
  between operations  9.15 us (1%)
    unnamed x25, blocking collectives  164 us
    ppermute x16, starting transfers between devices, with_halo(): lax.ppermute(lax.slice_in_dim(block, block.shape[dim] - width, None, axis...  66.2 us
    unnamed x117, local copies, waits for them, and re-layouts  57.6 us
    ppermute x16, starting transfers between devices, with_halo(): lax.ppermute(lax.slice_in_dim(block, 0, width, axis=dim), axis, backward)  43.5 us
    slice x12, local copies, waits for them, and re-layouts, split_axis(): lax.slice_in_dim(values, corner, corner + 2 * half_len - 1, stride=2, axi...  41.9 us
    reduce_sum x30, other arithmetic, over_axes(): shard = jnp.sum(lax.all_gather(shard, axis), axis=0)  18.2 us
    ppermute x16, waiting for transfers between devices, with_halo(): lax.ppermute(lax.slice_in_dim(block, block.shape[dim] - width, None, axis...  17.2 us
    dot_general x4, matrix products, split_nodes(): jnp.einsum('baqxyk,ckg->cbaqxyg', stacked, table, precision=lax.Precision...  17.1 us
  transfers between devices with their start and end apart: 33, of which 14 were waited for; matrix products, arithmetic and copies ran while one was open for 8% of the time, Pallas kernels for 0%

profile of v1, /device:TPU:39, one launch (start us, length us, event | category | flops | bytes accessed | tf_op | source)
XLA Modules:
  0.0 613.8 jit_solution(14274410766484871311)
XLA Ops:
  4.3 7.1 %collective-permute-start = (f32[4,256,2]{2,1,0:T(8,128)}, f32[4,256,2]{2,1,0:T(8,128)}, u32[]{:S(2)}, u32[]{:S(2)}) collective-permute-start(f32[4,256,2]{2,1,0:T(8,128)} %get-tuple-element.92), channel_id=1, source_target_pairs={{0,64},{1,65},{2,66},{3,67},{4,68},{5,69},{6,70},{7,71},{8,72},{9,... | collective-permute-start | bytes 24584 | tf_op jit(solution)/shard_map/ppermute | solution.py:23
  16.1 5.5 collective-permute-start.4
  28.7 4.3 collective-permute-start.6
  47.0 6.1 collective-permute-start.2
  60.2 5.8 slice.538
  66.0 5.7 slice.537
  71.6 5.7 slice.536
  82.2 5.7 reduce_sum.350
  92.9 4.5 all-to-all-start
  97.4 4.4 fusion.40
  107.2 3.9 fusion.3
  111.0 3.3 reshape.253
  129.4 5.5 collective-permute-start.10
  140.2 4.3 collective-permute-start.12
  146.9 5.1 collective-permute-start.15
  165.2 5.8 all-reduce.49
  175.7 8.5 %all-reduce.46 = (f32[4]{0:T(128)S(1)}, f32[4]{0:T(128)S(1)}) all-reduce(f32[4]{0:T(128)S(1)} %dynamic-update-slice.1, f32[4]{0:T(128)S(1)} %dynamic-update-slice.6), channel_id=1, replica_groups=mesh['role'=2,'gx_0'=4,'gx_1'=2,'gy_0'=4,'gy_1'=2] {'gx_0'}, use_global_device_ids=true, to_apply=%add.16 | all-reduce | flops 8 | bytes 64
  188.7 5.4 all-reduce.48
  198.8 5.7 all-reduce.45
  208.6 9.3 %all-reduce.47 = (f32[2]{0:T(128)S(1)}, f32[2]{0:T(128)S(1)}) all-reduce(f32[2]{0:T(128)S(1)} %dynamic-update-slice.4, f32[2]{0:T(128)S(1)} %dynamic-update-slice.9), channel_id=1, replica_groups=mesh['role'=2,'gx_0'=4,'gx_1'=2,'gy_0'=4,'gy_1'=2] {'gy_1'}, use_global_device_ids=true, to_apply=%add.19 | all-reduce | flops 4 | bytes 32
  225.3 5.3 all-reduce.25
  232.6 6.0 all-reduce.26
  240.5 4.3 all-reduce.27
  246.7 8.0 %all-reduce.28 = f32[4]{0:T(128)S(1)} all-reduce(f32[4]{0:T(128)S(1)} %dynamic-update-slice.13), channel_id=1, replica_groups=mesh['role'=2,'gx_0'=4,'gx_1'=2,'gy_0'=4,'gy_1'=2] {'gy_0'}, use_global_device_ids=true, to_apply=%add.28 | all-reduce | flops 4 | bytes 32
  256.7 8.3 %all-reduce.29 = f32[2]{0:T(128)S(1)} all-reduce(f32[2]{0:T(128)S(1)} %dynamic-update-slice.14), channel_id=1, replica_groups=mesh['role'=2,'gx_0'=4,'gx_1'=2,'gy_0'=4,'gy_1'=2] {'gy_1'}, use_global_device_ids=true, to_apply=%add.29 | all-reduce | flops 2 | bytes 16
  267.0 3.5 slice_multiply_fusion.26
  272.1 4.9 slice.572
  277.0 5.7 slice.571
  282.7 5.7 slice.570
  288.4 4.4 fusion.39
  292.7 3.3 reshape.256
  296.0 3.9 fusion.2
  299.9 3.3 reshape.257
  318.4 5.5 collective-permute-start.16
  327.2 3.7 collective-permute-start.19
  330.9 3.4 collective-permute-start.18
  336.9 4.3 collective-permute-start.21
  350.6 5.3 all-reduce.30
  357.9 7.7 %all-reduce.31 = f32[4]{0:T(128)S(1)} all-reduce(f32[4]{0:T(128)S(1)} %dynamic-update-slice.16), channel_id=1, replica_groups=mesh['role'=2,'gx_0'=4,'gx_1'=2,'gy_0'=4,'gy_1'=2] {'gx_0'}, use_global_device_ids=true, to_apply=%add.31 | all-reduce | flops 4 | bytes 32
  367.6 3.8 all-reduce.32
  373.4 7.3 %all-reduce.33 = f32[4]{0:T(128)S(1)} all-reduce(f32[4]{0:T(128)S(1)} %dynamic-update-slice.18), channel_id=1, replica_groups=mesh['role'=2,'gx_0'=4,'gx_1'=2,'gy_0'=4,'gy_1'=2] {'gy_0'}, use_global_device_ids=true, to_apply=%add.33 | all-reduce | flops 4 | bytes 32
  382.8 9.0 %all-reduce.34 = f32[2]{0:T(128)S(1)} all-reduce(f32[2]{0:T(128)S(1)} %dynamic-update-slice.19), channel_id=1, replica_groups=mesh['role'=2,'gx_0'=4,'gx_1'=2,'gy_0'=4,'gy_1'=2] {'gy_1'}, use_global_device_ids=true, to_apply=%add.34 | all-reduce | flops 2 | bytes 16
  398.6 5.3 all-reduce.35
  405.9 6.2 %all-reduce.36 = f32[4]{0:T(128)S(1)} all-reduce(f32[4]{0:T(128)S(1)} %dynamic-update-slice.21), channel_id=1, replica_groups=mesh['role'=2,'gx_0'=4,'gx_1'=2,'gy_0'=4,'gy_1'=2] {'gx_0'}, use_global_device_ids=true, to_apply=%add.36 | all-reduce | flops 4 | bytes 32
  414.2 4.3 all-reduce.37
  420.5 7.9 %all-reduce.38 = f32[4]{0:T(128)S(1)} all-reduce(f32[4]{0:T(128)S(1)} %dynamic-update-slice.23), channel_id=1, replica_groups=mesh['role'=2,'gx_0'=4,'gx_1'=2,'gy_0'=4,'gy_1'=2] {'gy_0'}, use_global_device_ids=true, to_apply=%add.38 | all-reduce | flops 4 | bytes 32
  430.4 8.2 %all-reduce.39 = f32[2]{0:T(128)S(1)} all-reduce(f32[2]{0:T(128)S(1)} %dynamic-update-slice.24), channel_id=1, replica_groups=mesh['role'=2,'gx_0'=4,'gx_1'=2,'gy_0'=4,'gy_1'=2] {'gy_1'}, use_global_device_ids=true, to_apply=%add.39 | all-reduce | flops 2 | bytes 16
  448.2 4.2 fusion.38
  457.4 3.3 reshape.261
  472.9 5.5 collective-permute-start.22
  479.9 3.7 collective-permute-start.25
  489.0 4.8 collective-permute-start.27
  502.4 5.3 all-reduce.40
  509.6 6.3 %all-reduce.41 = f32[4]{0:T(128)S(1)} all-reduce(f32[4]{0:T(128)S(1)} %dynamic-update-slice.26), channel_id=1, replica_groups=mesh['role'=2,'gx_0'=4,'gx_1'=2,'gy_0'=4,'gy_1'=2] {'gx_0'}, use_global_device_ids=true, to_apply=%add.41 | all-reduce | flops 4 | bytes 32
  517.8 4.9 all-reduce.42
  524.6 7.5 %all-reduce.43 = f32[4]{0:T(128)S(1)} all-reduce(f32[4]{0:T(128)S(1)} %dynamic-update-slice.28), channel_id=1, replica_groups=mesh['role'=2,'gx_0'=4,'gx_1'=2,'gy_0'=4,'gy_1'=2] {'gy_0'}, use_global_device_ids=true, to_apply=%add.43 | all-reduce | flops 4 | bytes 32
  534.0 8.3 %all-reduce.44 = f32[2]{0:T(128)S(1)} all-reduce(f32[2]{0:T(128)S(1)} %dynamic-update-slice.29), channel_id=1, replica_groups=mesh['role'=2,'gx_0'=4,'gx_1'=2,'gy_0'=4,'gy_1'=2] {'gy_1'}, use_global_device_ids=true, to_apply=%add.44 | all-reduce | flops 2 | bytes 16
  551.2 4.2 fusion.37
  559.5 8.7 %all_to_all.21 = f32[8,1,512]{2,1,0:T(1,128)S(1)} all-to-all(f32[8,1,512]{2,1,0:T(1,128)S(1)} %reshape.436), channel_id=1, replica_groups=mesh['role'=2,'gx_0'=4,'gx_1'=2,'gy_0'=4,'gy_1'=2] {'gy_0','gy_1'}, dimensions={0} | all-to-all | bytes 32768 | tf_op jit(solution)/shard_map/all_to_all | solution.py:254
  571.7 5.0 mul.384
  578.5 5.6 collective-permute-start.28
  584.1 9.3 %collective-permute-done.29 = f32[4,256,2]{2,1,0:T(8,128)S(1)} collective-permute-done((f32[4,256,2]{2,1,0:T(8,128)S(1)}, f32[4,256,2]{2,1,0:T(8,128)S(1)}, u32[]{:S(2)}, u32[]{:S(2)}) %collective-permute-start.29) | collective-permute-done | bytes 8224 | tf_op jit(solution)/shard_map/ppermute | solution.py:26
  594.8 4.1 collective-permute-start.31
  598.9 5.4 collective-permute-start.30
  (380 shorter events, 249.2 us)
Async XLA Ops:
  0.6 106.5 %copy-start = (f32[81,81]{1,0:T(8,128)S(1)}, f32[81,81]{1,0:T(8,128)}, u32[]{:S(2)}) copy-start(f32[81,81]{1,0:T(8,128)} %param.7) | copy-start | bytes 78736
  0.6 10.8 %copy-start.20 = (s32[3,16,16,128]{3,2,1,0:T(8,128)S(1)}, s32[3,16,16,128]{3,2,1,0:T(8,128)}, u32[]{:S(2)}) copy-start(s32[3,16,16,128]{3,2,1,0:T(8,128)} %param.6) | copy-start | bytes 1179652
  0.7 10.8 %copy-start.19 = (f32[3,16,16,128]{3,2,1,0:T(8,128)S(1)}, f32[3,16,16,128]{3,2,1,0:T(8,128)}, u32[]{:S(2)}) copy-start(f32[3,16,16,128]{3,2,1,0:T(8,128)} %param.5) | copy-start | bytes 1179652
  3.1 29.9 %collective-permute-start.1 = (f32[4,256,2]{2,1,0:T(8,128)}, f32[4,256,2]{2,1,0:T(8,128)}, u32[]{:S(2)}, u32[]{:S(2)}) collective-permute-start(f32[4,256,2]{2,1,0:T(8,128)} %get-tuple-element.93), channel_id=1, source_target_pairs={{64,0},{65,1},{66,2},{67,3},{68,4},{69,5},{70,6},{71,7},{72,8},{73... | collective-permute-start | bytes 24584 | tf_op jit(solution)/shard_map/ppermute | solution.py:26
  4.3 28.6 %collective-permute-start = (f32[4,256,2]{2,1,0:T(8,128)}, f32[4,256,2]{2,1,0:T(8,128)}, u32[]{:S(2)}, u32[]{:S(2)}) collective-permute-start(f32[4,256,2]{2,1,0:T(8,128)} %get-tuple-element.92), channel_id=1, source_target_pairs={{0,64},{1,65},{2,66},{3,67},{4,68},{5,69},{6,70},{7,71},{8,72},{9,... | collective-permute-start | bytes 24584 | tf_op jit(solution)/shard_map/ppermute | solution.py:23
  14.8 7.0 %collective-permute-start.5 = (f32[6,17,17,1]{2,3,1,0:T(1,128)S(1)}, f32[6,17,17,1]{2,3,1,0:T(1,128)S(1)}, u32[]{:S(2)}, u32[]{:S(2)}) collective-permute-start(f32[6,17,17,1]{2,3,1,0:T(1,128)S(1)} %copy.52), channel_id=1, source_target_pairs={{64,0},{65,1},{66,2},{67,3},{68,4},{69,5},{70,6},{71,7},{72,8},{73... | collective-permute-start | bytes 20816 | tf_op jit(solution)/shard_map/ppermute | solution.py:26
  16.1 7.4 %collective-permute-start.4 = (f32[6,17,17,1]{2,3,1,0:T(1,128)S(1)}, f32[6,17,17,1]{2,3,1,0:T(1,128)S(1)}, u32[]{:S(2)}, u32[]{:S(2)}) collective-permute-start(f32[6,17,17,1]{2,3,1,0:T(1,128)S(1)} %slice.514), channel_id=1, source_target_pairs={{0,64},{1,65},{2,66},{3,67},{4,68},{5,69},{6,70},{7,71},{8,72},{9,... | collective-permute-start | bytes 20816 | tf_op jit(solution)/shard_map/ppermute | solution.py:23
  25.3 7.6 %copy-start.13 = (f32[4,256,128]{2,1,0:T(8,128)S(1)}, f32[4,256,128]{2,1,0:T(8,128)}, u32[]{:S(2)}) copy-start(f32[4,256,128]{2,1,0:T(8,128)} %param.4) | copy-start | bytes 1572868
  26.6 11.1 %copy-start.1 = (f32[6,17,17,1]{3,2,1,0:T(8,128)S(1)}, f32[6,17,17,1]{3,2,1,0:T(8,128)}, u32[]{:S(2)}) copy-start(f32[6,17,17,1]{3,2,1,0:T(8,128)} %copy.54) | copy-start | bytes 20812
  26.6 11.1 %copy-start.2 = (f32[6,17,17,1]{3,2,1,0:T(8,128)S(1)}, f32[6,17,17,1]{3,2,1,0:T(8,128)}, u32[]{:S(2)}) copy-start(f32[6,17,17,1]{3,2,1,0:T(8,128)} %copy.53) | copy-start | bytes 20812
  26.6 8.1 %collective-permute-start.7 = (f32[6,1,17,131]{3,2,1,0:T(8,128)S(1)}, f32[6,1,17,131]{3,2,1,0:T(8,128)S(1)}, u32[]{:S(2)}, u32[]{:S(2)}) collective-permute-start(f32[6,1,17,131]{3,2,1,0:T(8,128)S(1)} %get-tuple-element.25), channel_id=1, source_target_pairs={{8,0},{16,8},{24,16},{32,24},{40,32},{48,40},{56,48},{9,1},{17,9},... | collective-permute-start | bytes 160352 | tf_op jit(solution)/shard_map/ppermute | solution.py:26
  28.7 9.0 %collective-permute-start.6 = (f32[6,1,17,131]{3,2,1,0:T(8,128)S(1)}, f32[6,1,17,131]{3,2,1,0:T(8,128)S(1)}, u32[]{:S(2)}, u32[]{:S(2)}) collective-permute-start(f32[6,1,17,131]{3,2,1,0:T(8,128)S(1)} %get-tuple-element.24), channel_id=1, source_target_pairs={{0,8},{8,16},{16,24},{24,32},{32,40},{40,48},{48,56},{1,9},{9,17},... | collective-permute-start | bytes 160352 | tf_op jit(solution)/shard_map/ppermute | solution.py:23
  38.4 14.6 %collective-permute-start.9 = (f32[6,19,1,131]{3,2,1,0:T(1,128)S(1)}, f32[6,19,1,131]{3,2,1,0:T(1,128)S(1)}, u32[]{:S(2)}, u32[]{:S(2)}) collective-permute-start(f32[6,19,1,131]{3,2,1,0:T(1,128)S(1)} %get-tuple-element.23), channel_id=1, source_target_pairs={{1,0},{2,1},{3,2},{4,3},{5,4},{6,5},{7,6},{9,8},{10,9},{11,10},{12... | collective-permute-start | bytes 179216 | tf_op jit(solution)/shard_map/ppermute | solution.py:26
  41.6 11.5 %collective-permute-start.8 = (f32[6,19,1,131]{3,2,1,0:T(1,128)S(1)}, f32[6,19,1,131]{3,2,1,0:T(1,128)S(1)}, u32[]{:S(2)}, u32[]{:S(2)}) collective-permute-start(f32[6,19,1,131]{3,2,1,0:T(1,128)S(1)} %get-tuple-element.22), channel_id=1, source_target_pairs={{0,1},{1,2},{2,3},{3,4},{4,5},{5,6},{6,7},{8,9},{9,10},{10,11},{11... | collective-permute-start | bytes 179216 | tf_op jit(solution)/shard_map/ppermute | solution.py:23
  43.9 33.4 %collective-permute-start.3 = (f32[2,256,132]{2,1,0:T(8,128)}, f32[2,256,132]{2,1,0:T(8,128)}, u32[]{:S(2)}, u32[]{:S(2)}) collective-permute-start(f32[2,256,132]{2,1,0:T(8,128)} %get-tuple-element.89), channel_id=1, source_target_pairs={{1,0},{2,1},{3,2},{4,3},{5,4},{6,5},{7,6},{8,7},{9,8},{10,9},{11,1... | collective-permute-start | bytes 811016 | tf_op jit(solution)/shard_map/ppermute | solution.py:26
  47.0 30.3 %collective-permute-start.2 = (f32[2,256,132]{2,1,0:T(8,128)}, f32[2,256,132]{2,1,0:T(8,128)}, u32[]{:S(2)}, u32[]{:S(2)}) collective-permute-start(f32[2,256,132]{2,1,0:T(8,128)} %get-tuple-element.88), channel_id=1, source_target_pairs={{0,1},{1,2},{2,3},{3,4},{4,5},{5,6},{6,7},{7,8},{8,9},{9,10},{10,1... | collective-permute-start | bytes 811016 | tf_op jit(solution)/shard_map/ppermute | solution.py:23
  87.9 9.5 %copy-start.17 = (f32[3,3,8,8,129]{4,3,2,1,0:T(8,128)S(1)}, f32[3,3,8,8,129]{4,3,2,1,0:T(8,128)}, u32[]{:S(2)}) copy-start(f32[3,3,8,8,129]{4,3,2,1,0:T(8,128)} %slice.538) | copy-start | bytes 891652
  92.9 12.1 %all-to-all-start = ((f32[8,1,512]{2,1,0:T(1,128)}), f32[8,1,512]{2,1,0:T(1,128)S(1)}, u32[]{:S(2)}, u32[]{:S(2)}) async-start(f32[8,1,512]{2,1,0:T(1,128)} %reshape.434), calls=%async_computation | async-start | bytes 32768 | tf_op jit(solution)/shard_map/all_to_all | solution.py:222
  124.3 1.0 copy-start.3
  127.7 7.2 %collective-permute-start.11 = (f32[3,17,17,1]{2,3,1,0:T(1,128)S(1)}, f32[3,17,17,1]{2,3,1,0:T(1,128)S(1)}, u32[]{:S(2)}, u32[]{:S(2)}) collective-permute-start(f32[3,17,17,1]{2,3,1,0:T(1,128)S(1)} %copy.64), channel_id=1, source_target_pairs={{64,0},{65,1},{66,2},{67,3},{68,4},{69,5},{70,6},{71,7},{72,8},{73... | collective-permute-start | bytes 10412 | tf_op jit(solution)/shard_map/ppermute | solution.py:26
  129.4 6.4 %collective-permute-start.10 = (f32[3,17,17,1]{2,3,1,0:T(1,128)S(1)}, f32[3,17,17,1]{2,3,1,0:T(1,128)S(1)}, u32[]{:S(2)}, u32[]{:S(2)}) collective-permute-start(f32[3,17,17,1]{2,3,1,0:T(1,128)S(1)} %copy.63), channel_id=1, source_target_pairs={{0,64},{1,65},{2,66},{3,67},{4,68},{5,69},{6,70},{7,71},{8,72},{9,... | collective-permute-start | bytes 10412 | tf_op jit(solution)/shard_map/ppermute | solution.py:23
  137.1 8.8 %copy-start.4 = (f32[3,8,2,17,129]{4,3,2,1,0:T(8,128)S(1)}, f32[3,8,2,17,129]{4,3,2,1,0:T(8,128)}, u32[]{:S(2)}) copy-start(f32[3,8,2,17,129]{4,3,2,1,0:T(8,128)} %copy-done.3) | copy-start | bytes 1263172
  137.1 8.8 %copy-start.10 = (f32[3,17,17,1]{3,2,1,0:T(8,128)S(1)}, f32[3,17,17,1]{3,2,1,0:T(8,128)}, u32[]{:S(2)}) copy-start(f32[3,17,17,1]{3,2,1,0:T(8,128)} %copy.65) | copy-start | bytes 10408
  138.3 15.3 %copy-start.25 = (u32[128]{0:T(128)S(1)}, u32[128]{0:T(128)}, u32[]{:S(2)}) copy-start(u32[128]{0:T(128)} %constant.144) | copy-start | bytes 1540
  138.3 6.2 %collective-permute-start.13 = (f32[3,1,17,131]{3,2,1,0:T(8,128)S(1)}, f32[3,1,17,131]{3,2,1,0:T(8,128)S(1)}, u32[]{:S(2)}, u32[]{:S(2)}) collective-permute-start(f32[3,1,17,131]{3,2,1,0:T(8,128)S(1)} %get-tuple-element.38), channel_id=1, source_target_pairs={{8,0},{16,8},{24,16},{32,24},{40,32},{48,40},{56,48},{9,1},{17,9},... | collective-permute-start | bytes 80180 | tf_op jit(solution)/shard_map/ppermute | solution.py:26
  140.2 5.7 collective-permute-start.12
  146.9 7.2 %collective-permute-start.15 = (f32[3,19,1,131]{3,2,1,0:T(1,128)}, f32[3,19,1,131]{3,2,1,0:T(1,128)}, u32[]{:S(2)}, u32[]{:S(2)}) collective-permute-start(f32[3,19,1,131]{3,2,1,0:T(1,128)} %get-tuple-element.31), channel_id=1, source_target_pairs={{1,0},{2,1},{3,2},{4,3},{5,4},{6,5},{7,6},{9,8},{10,9},{11,10},{12... | collective-permute-start | bytes 89612 | tf_op jit(solution)/shard_map/ppermute | solution.py:26
  152.0 3.3 collective-permute-start.14
  157.9 6.6 %copy-start.24 = (u32[128]{0:T(128)S(1)}, u32[128]{0:T(128)}, u32[]{:S(2)}) copy-start(u32[128]{0:T(128)} %constant.149) | copy-start | bytes 1540
  157.9 17.2 %copy-start.23 = (u32[128]{0:T(128)S(1)}, u32[128]{0:T(128)}, u32[]{:S(2)}) copy-start(u32[128]{0:T(128)} %constant.154) | copy-start | bytes 1540
  158.0 30.2 %copy-start.22 = (u32[128]{0:T(128)S(1)}, u32[128]{0:T(128)}, u32[]{:S(2)}) copy-start(u32[128]{0:T(128)} %constant.159) | copy-start | bytes 1540
  158.0 40.2 %copy-start.21 = (u32[128]{0:T(128)S(1)}, u32[128]{0:T(128)}, u32[]{:S(2)}) copy-start(u32[128]{0:T(128)} %constant.164) | copy-start | bytes 1540
  158.9 1.1 copy-start.15
  222.3 1.1 copy-start.9
  313.2 1.0 copy-start.5
  316.7 7.2 %collective-permute-start.17 = (f32[3,17,17,1]{2,3,1,0:T(1,128)S(1)}, f32[3,17,17,1]{2,3,1,0:T(1,128)S(1)}, u32[]{:S(2)}, u32[]{:S(2)}) collective-permute-start(f32[3,17,17,1]{2,3,1,0:T(1,128)S(1)} %copy.76), channel_id=1, source_target_pairs={{64,0},{65,1},{66,2},{67,3},{68,4},{69,5},{70,6},{71,7},{72,8},{73... | collective-permute-start | bytes 10412 | tf_op jit(solution)/shard_map/ppermute | solution.py:26
  318.4 6.4 %collective-permute-start.16 = (f32[3,17,17,1]{2,3,1,0:T(1,128)S(1)}, f32[3,17,17,1]{2,3,1,0:T(1,128)S(1)}, u32[]{:S(2)}, u32[]{:S(2)}) collective-permute-start(f32[3,17,17,1]{2,3,1,0:T(1,128)S(1)} %copy.75), channel_id=1, source_target_pairs={{0,64},{1,65},{2,66},{3,67},{4,68},{5,69},{6,70},{7,71},{8,72},{9,... | collective-permute-start | bytes 10412 | tf_op jit(solution)/shard_map/ppermute | solution.py:23
  326.0 10.5 %copy-start.6 = (f32[3,8,2,17,129]{4,3,2,1,0:T(8,128)S(1)}, f32[3,8,2,17,129]{4,3,2,1,0:T(8,128)}, u32[]{:S(2)}) copy-start(f32[3,8,2,17,129]{4,3,2,1,0:T(8,128)} %copy-done.5) | copy-start | bytes 1263172
  326.0 10.5 %copy-start.11 = (f32[3,17,17,1]{3,2,1,0:T(8,128)S(1)}, f32[3,17,17,1]{3,2,1,0:T(8,128)}, u32[]{:S(2)}) copy-start(f32[3,17,17,1]{3,2,1,0:T(8,128)} %copy.77) | copy-start | bytes 10408
  327.2 7.1 %collective-permute-start.19 = (f32[3,1,17,131]{3,2,1,0:T(8,128)S(1)}, f32[3,1,17,131]{3,2,1,0:T(8,128)S(1)}, u32[]{:S(2)}, u32[]{:S(2)}) collective-permute-start(f32[3,1,17,131]{3,2,1,0:T(8,128)S(1)} %get-tuple-element.36), channel_id=1, source_target_pairs={{8,0},{16,8},{24,16},{32,24},{40,32},{48,40},{56,48},{9,1},{17,9},... | collective-permute-start | bytes 80180 | tf_op jit(solution)/shard_map/ppermute | solution.py:26
  330.9 5.6 collective-permute-start.18
  336.9 5.8 collective-permute-start.21
  341.2 3.1 collective-permute-start.20
  346.5 1.1 copy-start.16
  395.5 1.1 copy-start.14
  471.2 7.2 %collective-permute-start.23 = (f32[3,17,17,1]{2,3,1,0:T(1,128)S(1)}, f32[3,17,17,1]{2,3,1,0:T(1,128)S(1)}, u32[]{:S(2)}, u32[]{:S(2)}) collective-permute-start(f32[3,17,17,1]{2,3,1,0:T(1,128)S(1)} %copy.88), channel_id=1, source_target_pairs={{64,0},{65,1},{66,2},{67,3},{68,4},{69,5},{70,6},{71,7},{72,8},{73... | collective-permute-start | bytes 10412 | tf_op jit(solution)/shard_map/ppermute | solution.py:26
  472.9 6.4 %collective-permute-start.22 = (f32[3,17,17,1]{2,3,1,0:T(1,128)S(1)}, f32[3,17,17,1]{2,3,1,0:T(1,128)S(1)}, u32[]{:S(2)}, u32[]{:S(2)}) collective-permute-start(f32[3,17,17,1]{2,3,1,0:T(1,128)S(1)} %copy.87), channel_id=1, source_target_pairs={{0,64},{1,65},{2,66},{3,67},{4,68},{5,69},{6,70},{7,71},{8,72},{9,... | collective-permute-start | bytes 10412 | tf_op jit(solution)/shard_map/ppermute | solution.py:23
  479.9 6.2 %collective-permute-start.25 = (f32[3,1,17,131]{3,2,1,0:T(8,128)S(1)}, f32[3,1,17,131]{3,2,1,0:T(8,128)S(1)}, u32[]{:S(2)}, u32[]{:S(2)}) collective-permute-start(f32[3,1,17,131]{3,2,1,0:T(8,128)S(1)} %get-tuple-element.34), channel_id=1, source_target_pairs={{8,0},{16,8},{24,16},{32,24},{40,32},{48,40},{56,48},{9,1},{17,9},... | collective-permute-start | bytes 80180 | tf_op jit(solution)/shard_map/ppermute | solution.py:26
  483.5 5.1 collective-permute-start.24
  489.0 6.3 %collective-permute-start.27 = (f32[3,19,1,131]{3,2,1,0:T(1,128)S(1)}, f32[3,19,1,131]{3,2,1,0:T(1,128)S(1)}, u32[]{:S(2)}, u32[]{:S(2)}) collective-permute-start(f32[3,19,1,131]{3,2,1,0:T(1,128)S(1)} %get-tuple-element.27), channel_id=1, source_target_pairs={{1,0},{2,1},{3,2},{4,3},{5,4},{6,5},{7,6},{9,8},{10,9},{11,10},{12... | collective-permute-start | bytes 89612 | tf_op jit(solution)/shard_map/ppermute | solution.py:26
  493.8 3.1 collective-permute-start.26
  498.2 46.0 %copy-start.7 = (f32[3,17,17,129]{3,2,1,0:T(8,128)S(1)}, f32[3,17,17,129]{3,2,1,0:T(8,128)}, u32[]{:S(2)}) copy-start(f32[3,17,17,129]{3,2,1,0:T(8,128)} %get-tuple-element.21) | copy-start | bytes 1342120
  498.2 46.0 %copy-start.8 = (f32[3,17,17,129]{3,2,1,0:T(8,128)S(1)}, f32[3,17,17,129]{3,2,1,0:T(8,128)}, u32[]{:S(2)}) copy-start(f32[3,17,17,129]{3,2,1,0:T(8,128)} %get-tuple-element.17) | copy-start | bytes 1342120
  545.8 1.0 copy-start.12
  571.7 5.1 copy-start.18
  577.2 16.1 %collective-permute-start.29 = (f32[4,256,2]{2,1,0:T(8,128)S(1)}, f32[4,256,2]{2,1,0:T(8,128)S(1)}, u32[]{:S(2)}, u32[]{:S(2)}) collective-permute-start(f32[4,256,2]{2,1,0:T(8,128)S(1)} %get-tuple-element.91), channel_id=1, source_target_pairs={{64,0},{65,1},{66,2},{67,3},{68,4},{69,5},{70,6},{71,7},{72,8},{73... | collective-permute-start | bytes 24584 | tf_op jit(solution)/shard_map/ppermute | solution.py:26
  578.5 15.7 %collective-permute-start.28 = (f32[4,256,2]{2,1,0:T(8,128)S(1)}, f32[4,256,2]{2,1,0:T(8,128)S(1)}, u32[]{:S(2)}, u32[]{:S(2)}) collective-permute-start(f32[4,256,2]{2,1,0:T(8,128)S(1)} %get-tuple-element.90), channel_id=1, source_target_pairs={{0,64},{1,65},{2,66},{3,67},{4,68},{5,69},{6,70},{7,71},{8,72},{9,... | collective-permute-start | bytes 24584 | tf_op jit(solution)/shard_map/ppermute | solution.py:23
  594.8 14.4 %collective-permute-start.31 = (f32[2,256,132]{2,1,0:T(8,128)S(1)}, f32[2,256,132]{2,1,0:T(8,128)S(1)}, u32[]{:S(2)}, u32[]{:S(2)}) collective-permute-start(f32[2,256,132]{2,1,0:T(8,128)S(1)} %get-tuple-element.87), channel_id=1, source_target_pairs={{1,0},{2,1},{3,2},{4,3},{5,4},{6,5},{7,6},{8,7},{9,8},{10,9},{11,1... | collective-permute-start | bytes 811016 | tf_op jit(solution)/shard_map/ppermute | solution.py:26
  598.9 11.5 %collective-permute-start.30 = (f32[2,256,132]{2,1,0:T(8,128)S(1)}, f32[2,256,132]{2,1,0:T(8,128)S(1)}, u32[]{:S(2)}, u32[]{:S(2)}) collective-permute-start(f32[2,256,132]{2,1,0:T(8,128)S(1)} %get-tuple-element.86), channel_id=1, source_target_pairs={{0,1},{1,2},{2,3},{3,4},{4,5},{5,6},{6,7},{7,8},{8,9},{9,10},{10,1... | collective-permute-start | bytes 811016 | tf_op jit(solution)/shard_map/ppermute | solution.py:23
